TPU v7x, 32 devices: a whole 2x2x4 slice. The times are simulated.
32 devices in a mesh: grid: 4 (over z), dom: 8 (over y, x, core).
Axes of the slice: x: 2, y: 2, z: 4, core: 2. Of those that a mesh axis runs over, the one named last changes fastest.
Arguments:
- nodal_values: float32 [8, 256, 8192], P('grid', None, 'dom'), may hold values from -6 to 6
- source_term: float32 [8, 256, 8192], P('grid', None, 'dom'), may hold values from -6 to 6
- velocity: float32 [8, 2], P('grid'), may hold values from 0.2 to 0.9
- react_rate: float32 [8], P('grid'), may hold values from 0.3 to 3
- levels: int32 [8, 2], P('grid'), may hold values from 5 to 8, as said below
- comb_coefs: int32 [8], P('grid'), may hold values from -1 to 1, as said below
Outputs:
- combined: float32 [8, 256, 8192], P('grid', None, 'dom')
Inputs may be any that keep to these rules, and one draw needn't show every extreme that they name: Each grid's two levels sum to 13 or 12. comb_coefs[c] is 1 where the levels of grid c sum to 13 and -1 where they sum to 12.
All inputs are finite; a program needn't handle non-finite values.
Results may differ from a plain program's by a relative error of at most 0.0003.
Values sent between devices are 32-bit elements; how exact they have to be, the bound alone decides.
No kernel may reach another device: no remote copies, remote signals or barrier semaphores. Data moves between devices by JAX's collectives and lax.ppermute only.
A program may use at most 64 MiB of HBM per device.

v0:
```python
import jax
import jax.numpy as jnp
import numpy as np
from jax import lax
from jax.sharding import PartitionSpec as P

MAXL = 8
LINE = 256
LSUM = 13
MINL = 5


tau_react = 0.25


def fine_order(line_depth):
    listing = [0]
    for tier_num in range(1, line_depth + 1):
        stride_len = 2 ** (line_depth - tier_num)
        listing.extend(range(stride_len, 2**line_depth, 2 * stride_len))
    return np.array(listing, np.int32)


def column_slots(line_depth, lowest_level, level_sum, dom_count):
    shift_bits = dom_count.bit_length() - 1
    slot_limit = []
    for column in range(2**line_depth // dom_count):
        least_level = lowest_level
        if column > 0:
            least_level = max(lowest_level, column.bit_length() + shift_bits)
        slot_limit.append(2 ** min(line_depth, level_sum - least_level))
    slot_limit = np.array(slot_limit, np.int32)
    starts = np.concatenate([np.zeros(1, np.int32), np.cumsum(slot_limit)[:-1]]).astype(np.int32)
    owners = np.repeat(np.arange(slot_limit.shape[0], dtype=np.int32), slot_limit)
    return (starts, owners)


def select_table(place_idx, source_len, grid_count):
    sources = jnp.arange(source_len, dtype=jnp.int32)[None, :, None]
    onehot = (place_idx[:, None, :] == sources).astype(jnp.float32)
    return jnp.broadcast_to(onehot, (grid_count, source_len, place_idx.shape[-1]))


def pick_last(source_arr, place_idx):
    table = select_table(place_idx, source_arr.shape[-1], source_arr.shape[0])
    return jnp.einsum("zrs,zsd->zrd", source_arr, table, precision=lax.Precision.HIGHEST)


def advect_line(values, line_base, position, line_len, courant):
    ahead = pick_last(values, line_base + (position + 1) % line_len)
    behind = pick_last(values, line_base + (position + line_len - 1) % line_len)
    return (
        values
        - 0.5 * courant * (ahead - behind)
        + 0.5 * courant * courant * (ahead - 2.0 * values + behind)
    )


def hier_gather(values, line_base, position, line_len, line_level, order_table):
    node_idx = jnp.right_shift(jnp.take(order_table, position), MAXL - line_level)
    spacing = jnp.bitwise_and(node_idx, -node_idx)
    centre = pick_last(values, line_base + node_idx)
    left_val = pick_last(values, line_base + (node_idx - spacing) % line_len)
    right_val = pick_last(values, line_base + (node_idx + spacing) % line_len)
    half_w = jnp.where(node_idx > 0, 0.5, 0.0)[:, None, :]
    return centre - half_w * (left_val + right_val)


def hat_matrix(line_base, position, line_len, line_level, is_live, order_table):
    node_idx = jnp.right_shift(jnp.take(order_table, position), MAXL - line_level)
    spacing = jnp.bitwise_and(node_idx, -node_idx)
    apart = jnp.abs(position[:, :, None] - node_idx[:, None, :])
    apart = jnp.minimum(apart, line_len[:, :, None] - apart)
    ratio = apart.astype(jnp.float32) / jnp.maximum(spacing, 1).astype(jnp.float32)[:, None, :]
    weight = jnp.where(node_idx[:, None, :] == 0, 1.0, jnp.maximum(0.0, 1.0 - ratio))
    same_line = line_base[:, :, None] == line_base[:, None, :]
    both_live = is_live[:, :, None] & is_live[:, None, :]
    return jnp.where(same_line & both_live, weight, 0.0)


def combine_grids(partial_sum):
    return lax.psum(partial_sum, "grid")


def local(nodal_values, source_term, velocity, react_rate, levels, comb_coefs):
    grids_here, other_rows, block_len = nodal_values.shape
    dom_count = lax.axis_size("dom")
    segment = block_len // dom_count
    top_level_index = lax.Precision.HIGHEST
    order_table = jnp.asarray(fine_order(MAXL))
    start_np, owner_np = column_slots(MAXL, MINL, LSUM, dom_count)
    slot_starts = jnp.asarray(start_np)
    slot_owner = jnp.asarray(owner_np)[None, :]
    slot_offset = jnp.asarray(np.arange(owner_np.shape[0], dtype=np.int32) - start_np[owner_np])[
        None, :
    ]
    cols_level = levels[:, 0:1]
    rows_level = levels[:, 1:2]
    unit_ints = jnp.ones_like(cols_level)
    col_count = jnp.left_shift(unit_ints, cols_level)
    row_count = jnp.left_shift(unit_ints, rows_level)
    live_count = col_count * row_count // dom_count
    rows_block = live_count // col_count
    cols_block = col_count // dom_count
    places = jnp.arange(block_len, dtype=jnp.int32)[None, :]
    is_live = places < live_count
    live_mask = is_live.astype(jnp.float32)[:, None, :]
    nu_cols = (velocity[:, 0:1] * col_count.astype(jnp.float32) / LINE)[:, :, None]
    nu_rows = (velocity[:, 1:2] * row_count.astype(jnp.float32) / LINE)[:, :, None]
    row_local = places // col_count
    col_pos = places % col_count
    row_base = row_local * col_count
    col_local = places // row_count
    row_pos = places % row_count
    col_base = col_local * row_count
    dest_dev = places // segment
    slot_pos = places % segment
    send_ok = slot_pos < rows_block * cols_block
    send_mask = send_ok.astype(jnp.float32)[:, None, :]
    row_send = slot_pos // cols_block
    col_send = slot_pos % cols_block
    moved = nodal_values * live_mask
    moved = advect_line(moved, row_base, col_pos, col_count, nu_cols)
    reacted = (
        moved * (1.0 - tau_react * react_rate)[:, None, None] + tau_react * source_term * live_mask
    )
    surplus = hier_gather(reacted, row_base, col_pos, col_count, cols_level, order_table)
    send_from = jnp.where(send_ok, row_send * col_count + dest_dev + dom_count * col_send, 0)
    outgoing = (pick_last(surplus, send_from) * send_mask).reshape(
        grids_here, other_rows, dom_count, segment
    )
    incoming = lax.all_to_all(outgoing, "dom", split_axis=2, concat_axis=2, tiled=True).reshape(
        grids_here, other_rows, block_len
    )
    recv_from = jnp.where(
        is_live, row_pos // rows_block * segment + row_pos % rows_block * cols_block + col_local, 0
    )
    columns = pick_last(incoming, recv_from) * live_mask
    columns = advect_line(columns, col_base, row_pos, row_count, nu_rows)
    surplus = hier_gather(columns, col_base, row_pos, row_count, rows_level, order_table)
    pack_ok = (slot_owner < cols_block) & (slot_offset < row_count)
    pack_from = jnp.where(pack_ok, slot_owner * row_count + slot_offset, 0)
    pack_weight = (comb_coefs.astype(jnp.float32)[:, None] * pack_ok.astype(jnp.float32))[
        :, None, :
    ]
    partial_sum = jnp.sum(pick_last(surplus, pack_from) * pack_weight, axis=0)
    total_sum = combine_grids(partial_sum)
    unpack_at = jnp.where(
        is_live, jnp.take(slot_starts, jnp.where(is_live, col_local, 0)) + row_pos, 0
    )
    unpack_table = select_table(unpack_at, total_sum.shape[-1], grids_here)
    gathered_result = (
        jnp.einsum("rs,zsd->zrd", total_sum, unpack_table, precision=top_level_index) * live_mask
    )
    row_hat_values = hat_matrix(col_base, row_pos, row_count, rows_level, is_live, order_table)
    gathered_result = jnp.einsum(
        "zsd,zbd->zsb", gathered_result, row_hat_values, precision=top_level_index
    )
    gathered_result = advect_line(gathered_result, col_base, row_pos, row_count, nu_rows)
    send_back = jnp.where(send_ok, col_send * row_count + dest_dev * rows_block + row_send, 0)
    outgoing = (pick_last(gathered_result, send_back) * send_mask).reshape(
        grids_here, other_rows, dom_count, segment
    )
    incoming = lax.all_to_all(outgoing, "dom", split_axis=2, concat_axis=2, tiled=True).reshape(
        grids_here, other_rows, block_len
    )
    back_from = jnp.where(
        is_live, col_pos % dom_count * segment + row_local * cols_block + col_pos // dom_count, 0
    )
    row_arrangement = pick_last(incoming, back_from) * live_mask
    column_hat_values = hat_matrix(row_base, col_pos, col_count, cols_level, is_live, order_table)
    return jnp.einsum("zsd,zbd->zsb", row_arrangement, column_hat_values, precision=top_level_index)


def solution(mesh):
    in_specs = (
        P("grid", None, "dom"),
        P("grid", None, "dom"),
        P("grid", None),
        P("grid"),
        P("grid", None),
        P("grid"),
    )
    out_specs = P("grid", None, "dom")
    return jax.shard_map(local, mesh=mesh, in_specs=in_specs, out_specs=out_specs, check_vma=False)
```

profile of v0, /device:TPU:1, one launch (start us, length us, event | category | flops | bytes accessed | tf_op | source)
XLA Modules:
  0.0 355.8 jit_solution(10070317216394521176)
XLA Ops:
  6.6 1.1 compare_reduce_fusion.1
  7.7 0.1 reduce
  7.8 0.1 fusion.176
  7.9 0.1 broadcast_select_fusion.1
  8.0 1.2 sign_reduce_fusion.1
  9.2 0.1 compare_convert_fusion
  9.2 1.1 compare_select_fusion.3
  10.3 12.6 %gather_fusion = s32[2048]{0:T(1024)S(1)} fusion(s32[32]{0:T(128)S(1)} %copy-done.1, s32[2048]{0:T(1024)S(1)} %bitcast_clamp_fusion.2), kind=kCustom, calls=%fused_computation.2 | custom fusion | bytes 24576 | tf_op jit(solution)/shard_map/jit(_take)/gather | solution.py:149
  23.0 0.4 fusion.158
  23.4 0.2 copy-done
  23.6 13.1 %gather_fusion.2 = s32[2048]{0:T(1024)S(1)} fusion(s32[256]{0:T(256)S(1)} %copy-done, s32[2048]{0:T(1024)S(1)} %bitcast_clamp_fusion), kind=kCustom, calls=%fused_computation.1.clone | custom fusion | bytes 24576 | tf_op jit(solution)/shard_map/jit(_take)/gather | solution.py:60
  36.8 0.4 fusion.157
  37.3 13.6 %gather_fusion.1 = s32[2048]{0:T(1024)S(1)} fusion(s32[256]{0:T(256)S(1)} %copy-done, s32[2048]{0:T(1024)S(1)} %bitcast_clamp_fusion.1), kind=kCustom, calls=%fused_computation.clone | custom fusion | bytes 24576 | tf_op jit(solution)/shard_map/jit(_take)/gather | solution.py:60
  50.9 0.2 multiply_reduce_fusion.1
  51.1 0.4 compare_select_fusion.4
  51.6 0.4 compare_select_fusion.5
  52.0 4.6 %fusion.129 = (s32[2,1024]{1,0:T(2,128)S(1)}, s32[2,1024]{1,0:T(2,128)S(1)}, s32[2,1024]{1,0:T(2,128)S(1)}, f32[2,1024]{1,0:T(2,128)S(1)}, s32[2,1024]{1,0:T(2,1...) fusion(s32[2,1024]{1,0:T(2,128)S(1)} %get-tuple-element.31, ...), kind=kLoop, calls=%fused_computation.191 | loop fusion | flops 346112 | bytes 184414 | tf_op jit(solution)/shard_map/add | solution.py:64
  56.7 4.3 %fusion.24 = f32[2,256,1024]{2,1,0:T(8,128)S(1)} fusion(s32[2,1024]{1,0:T(2,128)S(1)} %get-tuple-element.54, f32[2,256,1024]{2,1,0:T(8,128)S(1)} %copy-done.8, f32[2,1024]{1,0:T(2,128)S(1)} %get-tuple-element.78), kind=kOutput, calls=%fused_computation.45 | convolution fusion | flops 6445072384 | bytes 4210688 | tf_op jit(solution)/shard_map/zrs,zsd->zrd/dot_general | solution.py:46
  61.0 5.0 %multiply_add_fusion.1 = f32[2,256,1024]{2,1,0:T(8,128)S(1)} fusion(f32[2,256,1024]{2,1,0:T(8,128)S(1)} %copy-done.7, f32[2,256,1024]{2,1,0:T(8,128)S(1)} %fusion.24, f32[2,256,1024]{2,1,0:T(8,128)S(1)} %copy-done.8, s32[2,1024]{1,0:T(2,128)S(1)} %get-tuple-element.55, f32[2,1024]{1,0:T(2,128)S(1)} %broadcast_select_fusion.1, f32[2]{0:T(128)S(1)} %get-tuple-element.89, ...), kind=kOutput, calls=%fused_computation.124 | convolution fusion | flops 6451363840 | bytes 8413208 | tf_op jit(solution)/shard_map/zrs,zsd->zrd/dot_general | solution.py:46
  66.0 4.2 %fusion.27 = f32[2,256,1024]{2,1,0:T(8,128)S(1)} fusion(f32[2,256,1024]{2,1,0:T(8,128)S(1)} %multiply_add_fusion.1, s32[2,1024]{1,0:T(2,128)S(1)} %get-tuple-element.42), kind=kOutput, calls=%fused_computation.48 | convolution fusion | flops 6444548096 | bytes 4202496 | tf_op jit(solution)/shard_map/zrs,zsd->zrd/dot_general | solution.py:46
  70.2 4.2 %fusion.28 = f32[2,256,1024]{2,1,0:T(8,128)S(1)} fusion(f32[2,256,1024]{2,1,0:T(8,128)S(1)} %multiply_add_fusion.1, s32[2,1024]{1,0:T(2,128)S(1)} %get-tuple-element.41), kind=kOutput, calls=%fused_computation.49 | convolution fusion | flops 6444548096 | bytes 4202496 | tf_op jit(solution)/shard_map/zrs,zsd->zrd/dot_general | solution.py:46
  74.4 4.4 %fusion.26 = f32[2,256,1024]{2,1,0:T(8,128)S(1)} fusion(f32[2,256,1024]{2,1,0:T(8,128)S(1)} %multiply_add_fusion.1, s32[2,1024]{1,0:T(2,128)S(1)} %get-tuple-element.44), kind=kOutput, calls=%fused_computation.47 | convolution fusion | flops 6444548096 | bytes 4202496 | tf_op jit(solution)/shard_map/zrs,zsd->zrd/dot_general | solution.py:46
  78.8 4.4 %multiply_bitcast_fusion.1 = f32[2,32,8,8,128]{4,3,2,1,0:T(8,128)S(1)} fusion(s32[2,1024]{1,0:T(2,128)S(1)} %get-tuple-element.37, f32[2,256,1024]{2,1,0:T(8,128)S(1)} %fusion.26, f32[2,256,1024]{2,1,0:T(8,128)S(1)} %fusion.27, f32[2,256,1024]{2,1,0:T(8,128)S(1)} %fusion.28, f32[2,1024]{1,0:T(2,128)S(1)} %compare_convert_fusion, ...), kind=kOutput, calls=%fused_computation.120 | convolution fusion | flops 6446645248 | bytes 8413184 | tf_op jit(solution)/shard_map/zrs,zsd->zrd/dot_general | solution.py:46
  83.2 1.5 copy.38
  84.8 5.4 %all-to-all-start = ((f32[2,256,8,128]{3,1,0,2:T(8,128)}), f32[2,256,8,128]{3,1,0,2:T(8,128)S(1)}, u32[]{:S(2)}, u32[]{:S(2)}) async-start(f32[2,256,8,128]{3,1,0,2:T(8,128)} %bitcast.51), calls=%async_computation | async-start | bytes 4194304 | tf_op jit(solution)/shard_map/all_to_all | solution.py:132
  90.1 0.4 all-reduce.2.cloned.1.call-start
  90.6 0.1 add_select_fusion
  90.7 0.1 broadcast_select_fusion
  90.8 22.6 %all-to-all-done = f32[2,256,8,128]{3,1,0,2:T(8,128)S(1)} async-done(((f32[2,256,8,128]{3,1,0,2:T(8,128)}), f32[2,256,8,128]{3,1,0,2:T(8,128)S(1)}, u32[]{:S(2)}, u32[]{:S(2)}) %all-to-all-start) | async-done | bytes 2097184 | tf_op jit(solution)/shard_map/all_to_all | solution.py:132
  113.3 4.2 %fusion.30 = f32[2,256,1024]{2,1,0:T(8,128)S(1)} fusion(s32[2,1024]{1,0:T(2,128)S(1)} %get-tuple-element.58, f32[2,256,8,128]{3,1,0,2:T(8,128)S(1)} %all-to-all-done), kind=kOutput, calls=%fused_computation.51 | convolution fusion | flops 6444548096 | bytes 4202496 | tf_op jit(solution)/shard_map/zrs,zsd->zrd/dot_general | solution.py:46
  117.5 4.2 %fusion.17 = f32[2,256,1024]{2,1,0:T(8,128)S(1)} fusion(s32[2,1024]{1,0:T(2,128)S(1)} %get-tuple-element.56, f32[2,256,1024]{2,1,0:T(8,128)S(1)} %fusion.30, f32[2,1024]{1,0:T(2,128)S(1)} %get-tuple-element.78), kind=kOutput, calls=%fused_computation.32 | convolution fusion | flops 6445072384 | bytes 4210688 | tf_op jit(solution)/shard_map/zrs,zsd->zrd/dot_general | solution.py:46
  121.7 4.6 %multiply_add_fusion = f32[2,256,1024]{2,1,0:T(8,128)S(1)} fusion(f32[2,256,1024]{2,1,0:T(8,128)S(1)} %fusion.17, f32[2,256,1024]{2,1,0:T(8,128)S(1)} %fusion.30, s32[2,1024]{1,0:T(2,128)S(1)} %get-tuple-element.57, f32[2]{0:T(128)S(1)} %get-tuple-element.75, f32[2]{0:T(128)S(1)} %get-tuple-element.74, f32[2,1024]{1,0:T(2,128)S(1)} %get-tuple-element.78), kind=kOutput, calls=%fused_computation.119 | convolution fusion | flops 6449790976 | bytes 6307856 | tf_op jit(solution)/shard_map/zrs,zsd->zrd/dot_general | solution.py:46
  126.3 4.2 %fusion.32 = f32[2,256,1024]{2,1,0:T(8,128)S(1)} fusion(f32[2,256,1024]{2,1,0:T(8,128)S(1)} %multiply_add_fusion, s32[2,1024]{1,0:T(2,128)S(1)} %get-tuple-element.62), kind=kOutput, calls=%fused_computation.53 | convolution fusion | flops 6444548096 | bytes 4202496 | tf_op jit(solution)/shard_map/zrs,zsd->zrd/dot_general | solution.py:46
  130.5 4.2 %fusion.33 = f32[2,256,1024]{2,1,0:T(8,128)S(1)} fusion(f32[2,256,1024]{2,1,0:T(8,128)S(1)} %multiply_add_fusion, s32[2,1024]{1,0:T(2,128)S(1)} %get-tuple-element.63), kind=kOutput, calls=%fused_computation.54 | convolution fusion | flops 6444548096 | bytes 4202496 | tf_op jit(solution)/shard_map/zrs,zsd->zrd/dot_general | solution.py:46
  134.7 4.4 %fusion.31 = f32[2,256,1024]{2,1,0:T(8,128)S(1)} fusion(f32[2,256,1024]{2,1,0:T(8,128)S(1)} %multiply_add_fusion, s32[2,1024]{1,0:T(2,128)S(1)} %get-tuple-element.61), kind=kOutput, calls=%fused_computation.52 | convolution fusion | flops 6444548096 | bytes 4202496 | tf_op jit(solution)/shard_map/zrs,zsd->zrd/dot_general | solution.py:46
  139.2 12.5 %multiply_reduce_fusion = f32[256,2560]{1,0:T(8,128)} fusion(s32[2,2560]{1,0:T(2,128)S(1)} %add_select_fusion, f32[2,2560]{1,0:T(2,128)S(1)} %broadcast_select_fusion, f32[2,256,1024]{2,1,0:T(8,128)S(1)} %fusion.31, f32[2,256,1024]{2,1,0:T(8,128)S(1)} %fusion.32, f32[2,256,1024]{2,1,0:T(8,128)S(1)} %fusion.33, f32[2,1024]{1,0:T(2,128)S(1)} %get-tuple-element.28), kind=kOutput, calls=%fused_computation.59 | convolution fusion | flops 16114909184 | bytes 8962048 | tf_op jit(solution)/shard_map/zrs,zsd->zrd/dot_general | solution.py:46
  151.7 0.0 all-reduce.2.cloned.1.call-update
  151.7 106.4 %all-reduce.2.cloned.1.call-done = f32[256,2560]{1,0:T(8,128)} async-done(((f32[256,2560]{1,0:T(8,128)}), f32[256,2560]{1,0:T(8,128)}) %all-reduce.2.cloned.1.call-update) | async-done | bytes 2621456 | tf_op jit(solution)/shard_map/psum | solution.py:82
  258.2 11.8 %fusion = f32[2,1024,256]{2,1,0:T(8,128)S(1)} fusion(s32[2,1024]{1,0:T(2,128)S(1)} %get-tuple-element.59, f32[256,2560]{1,0:T(8,128)} %all-reduce.2.cloned.1.call-done), kind=kOutput, calls=%fused_computation.5 | convolution fusion | flops 16111370240 | bytes 4726784 | tf_op jit(solution)/shard_map/rs,zsd->zrd/dot_general | solution.py:153
  270.0 18.8 %fusion.22 = f32[2,256,1024]{2,1,0:T(8,128)S(1)} fusion(f32[2,1024]{1,0:T(2,128)S(1)} %get-tuple-element.60, s32[2]{0:T(128)S(1)} %get-tuple-element.22, s32[2,1024]{1,0:T(2,128)S(1)} %get-tuple-element.29, s32[2,1024]{1,0:T(2,128)S(1)} %get-tuple-element.66, s32[2,1024]{1,0:T(2,128)S(1)} %get-tuple-element.64, ...), kind=kOutput, calls=%fused_computation.44 | convolution fusion | flops 6470238208 | bytes 4239368 | tf_op jit(solution)/shard_map/zsd,zbd->zsb/dot_general | solution.py:156
  288.8 4.2 %fusion.18 = f32[2,256,1024]{2,1,0:T(8,128)S(1)} fusion(f32[2,256,1024]{2,1,0:T(8,128)S(1)} %fusion.22, s32[2,1024]{1,0:T(2,128)S(1)} %get-tuple-element.57), kind=kOutput, calls=%fused_computation.34 | convolution fusion | flops 6444548096 | bytes 4202496 | tf_op jit(solution)/shard_map/zrs,zsd->zrd/dot_general | solution.py:46
  293.0 4.2 %fusion.16 = f32[2,256,1024]{2,1,0:T(8,128)S(1)} fusion(f32[2,256,1024]{2,1,0:T(8,128)S(1)} %fusion.22, s32[2,1024]{1,0:T(2,128)S(1)} %get-tuple-element.56), kind=kOutput, calls=%fused_computation.31 | convolution fusion | flops 6444548096 | bytes 4202496 | tf_op jit(solution)/shard_map/zrs,zsd->zrd/dot_general | solution.py:46
  297.2 5.0 %multiply_bitcast_fusion = f32[2,32,8,8,128]{4,3,2,1,0:T(8,128)S(1)} fusion(s32[2,1024]{1,0:T(2,128)S(1)} %get-tuple-element.38, f32[2,256,1024]{2,1,0:T(8,128)S(1)} %fusion.16, f32[2,256,1024]{2,1,0:T(8,128)S(1)} %fusion.18, f32[2,256,1024]{2,1,0:T(8,128)S(1)} %fusion.22, f32[2]{0:T(128)S(1)} %get-tuple-element.75, f32[2]{0:T(128)S(1)} %get-tuple-element.74, ...), kind=kOutput, calls=%fused_computation.106 | convolution fusion | flops 6449266688 | bytes 8405008 | tf_op jit(solution)/shard_map/zrs,zsd->zrd/dot_general | solution.py:46
  302.2 1.5 copy.37
  303.8 4.4 %all-to-all-start.1 = ((f32[2,256,8,128]{3,1,0,2:T(8,128)}), f32[2,256,8,128]{3,1,0,2:T(8,128)S(1)}, u32[]{:S(2)}, u32[]{:S(2)}) async-start(f32[2,256,8,128]{3,1,0,2:T(8,128)} %bitcast.50), calls=%async_computation.1 | async-start | bytes 4194304 | tf_op jit(solution)/shard_map/all_to_all | solution.py:164
  308.2 23.2 %all-to-all-done.1 = f32[2,256,8,128]{3,1,0,2:T(8,128)S(1)} async-done(((f32[2,256,8,128]{3,1,0,2:T(8,128)}), f32[2,256,8,128]{3,1,0,2:T(8,128)S(1)}, u32[]{:S(2)}, u32[]{:S(2)}) %all-to-all-start.1) | async-done | bytes 2097184 | tf_op jit(solution)/shard_map/all_to_all | solution.py:164
  331.3 4.2 %fusion.35 = f32[2,256,1024]{2,1,0:T(8,128)S(1)} fusion(s32[2,1024]{1,0:T(2,128)S(1)} %get-tuple-element.53, f32[2,256,8,128]{3,1,0,2:T(8,128)S(1)} %all-to-all-done.1), kind=kOutput, calls=%fused_computation.56 | convolution fusion | flops 6444548096 | bytes 4202496 | tf_op jit(solution)/shard_map/zrs,zsd->zrd/dot_general | solution.py:46
  335.5 13.0 %fusion.20 = f32[2,256,1024]{2,1,0:T(8,128)} fusion(f32[2,1024]{1,0:T(2,128)S(1)} %get-tuple-element.46, s32[2]{0:T(128)S(1)} %get-tuple-element.19, s32[2,1024]{1,0:T(2,128)S(1)} %get-tuple-element.31, s32[2,1024]{1,0:T(2,128)S(1)} %get-tuple-element.67, s32[2,1024]{1,0:T(2,128)S(1)} %get-tuple-element.65, pred[2,1024]{1,0:T(4,128)(4,1)S(1)} %broadcast_compare_fusion, ...), kind=kOutput, calls=%fused_computation.43 | convolution fusion | flops 6470238208 | bytes 4239368 | tf_op jit(solution)/shard_map/zsd,zbd->zsb/dot_general | solution.py:172
  (34 shorter events, 0.2 us)
Async XLA Ops:
  6.5 3.8 %copy-start.1 = (s32[32]{0:T(128)S(1)}, s32[32]{0:T(128)}, u32[]{:S(2)}) copy-start(s32[32]{0:T(128)} %constant.161.clone) | copy-start | bytes 388
  23.0 0.7 copy-start
  37.2 13.7 %copy-start.4 = (s32[2,2]{1,0:T(2,128)S(1)}, s32[2,2]{1,0:T(2,128)}, u32[]{:S(2)}) copy-start(s32[2,2]{1,0:T(2,128)} %param.22) | copy-start | bytes 52
  37.2 13.7 %copy-start.5 = (f32[2,2]{1,0:T(2,128)S(1)}, f32[2,2]{1,0:T(2,128)}, u32[]{:S(2)}) copy-start(f32[2,2]{1,0:T(2,128)} %param.20) | copy-start | bytes 52
  37.3 14.8 %copy-start.6 = (f32[2]{0:T(128)S(1)}, f32[2]{0:T(128)}, u32[]{:S(2)}) copy-start(f32[2]{0:T(128)} %param.21) | copy-start | bytes 28
  37.3 19.4 %copy-start.8 = (f32[2,256,1024]{2,1,0:T(8,128)S(1)}, f32[2,256,1024]{2,1,0:T(8,128)}, u32[]{:S(2)}) copy-start(f32[2,256,1024]{2,1,0:T(8,128)} %param.18) | copy-start | bytes 6291460
  56.7 4.3 %copy-start.7 = (f32[2,256,1024]{2,1,0:T(8,128)S(1)}, f32[2,256,1024]{2,1,0:T(8,128)}, u32[]{:S(2)}) copy-start(f32[2,256,1024]{2,1,0:T(8,128)} %param.19) | copy-start | bytes 6291460
  84.7 5.8 %copy-start.9 = (s32[2]{0:T(128)S(1)}, s32[2]{0:T(128)}, u32[]{:S(2)}) copy-start(s32[2]{0:T(128)} %param.23) | copy-start | bytes 28
  84.8 5.8 %copy-start.2 = (s32[2560]{0:T(1024)S(1)}, s32[2560]{0:T(1024)}, u32[]{:S(2)}) copy-start(s32[2560]{0:T(1024)} %constant.162.clone) | copy-start | bytes 30724
  84.8 5.8 %copy-start.3 = (s32[2560]{0:T(1024)S(1)}, s32[2560]{0:T(1024)}, u32[]{:S(2)}) copy-start(s32[2560]{0:T(1024)} %constant.163.clone) | copy-start | bytes 30724
  84.8 28.5 %all-to-all-start = ((f32[2,256,8,128]{3,1,0,2:T(8,128)}), f32[2,256,8,128]{3,1,0,2:T(8,128)S(1)}, u32[]{:S(2)}, u32[]{:S(2)}) async-start(f32[2,256,8,128]{3,1,0,2:T(8,128)} %bitcast.51), calls=%async_computation | async-start | bytes 4194304 | tf_op jit(solution)/shard_map/all_to_all | solution.py:132
  90.1 168.0 %all-reduce.2.cloned.1.call-start = ((), (), s32[]{:S(2)}) async-start(), calls=%async_computation.2 | async-start | bytes 5242880 | tf_op jit(solution)/shard_map/psum | solution.py:82
  303.8 27.6 %all-to-all-start.1 = ((f32[2,256,8,128]{3,1,0,2:T(8,128)}), f32[2,256,8,128]{3,1,0,2:T(8,128)S(1)}, u32[]{:S(2)}, u32[]{:S(2)}) async-start(f32[2,256,8,128]{3,1,0,2:T(8,128)} %bitcast.50), calls=%async_computation.1 | async-start | bytes 4194304 | tf_op jit(solution)/shard_map/all_to_all | solution.py:164
Sparse Core Ops, SparseCore 0:
  151.8 106.2 all-reduce.1
where the time goes:
time: 363 us; the launch traced here: 356 us
  waiting for transfers between devices  152 us (42%)
  matrix products  126 us (35%)
  local copies, waits for them, and re-layouts  42.7 us (12%)
  between operations  14.2 us (4%)
  other arithmetic  10.5 us (3%)
  starting transfers between devices  10.1 us (3%)
    psum x1, waiting for transfers between devices, combine_grids(): return lax.psum(partial_sum, 'grid')  106 us
    dot_general x17, matrix products, pick_last(): jnp.einsum('zrs,zsd->zrd', source_arr, table, precision=lax.Precision.HIG...  82.4 us
    all_to_all x2, waiting for transfers between devices, local(): lax.all_to_all(outgoing, 'dom', split_axis=2, concat_axis=2, tiled=True)  45.7 us
    gather x4, local copies, waits for them, and re-layouts, hier_gather(): jnp.take(order_table, position)  26.8 us
    dot_general x1, matrix products, local(): jnp.einsum('zsd,zbd->zsb', gathered_result, row_hat_values, precision=top...  18.8 us
    dot_general x1, matrix products, local(): jnp.einsum('zsd,zbd->zsb', row_arrangement, column_hat_values, precision=...  13 us
    gather x2, local copies, waits for them, and re-layouts, local(): jnp.take(slot_starts, jnp.where(is_live, col_local, 0)) + row_pos  12.6 us
    dot_general x1, matrix products, local(): jnp.einsum('rs,zsd->zrd', total_sum, unpack_table, precision=top_level_in...  11.8 us
  transfers between devices with their start and end apart: 3, of which 3 were waited for; matrix products, arithmetic and copies ran while one was open for 0% of the time, Pallas kernels for 0%

commit v1 on v0

v1 whole, which is shorter than its diff:
```python
import functools

import jax
import jax.numpy as jnp
import numpy as np
from jax import lax
from jax.experimental import pallas as pl
from jax.experimental.pallas import tpu as pltpu
from jax.sharding import PartitionSpec as P

MAXL = 8
MINL = 5
LSUM = 13
LINE = 2**MAXL
BASE = 2**MINL
TAU = 0.25
VMEM_BYTES = 48 * 2**20
EXACT = lax.Precision.HIGHEST

GROUPS = [(b, y) for b in range(MINL, MAXL + 1) for y in range(MINL, LSUM - b + 1)]
BAND_UNITS = [1] + [2**t for t in range(MAXL - MINL)]
BAND_FIRST = [0] + [2**t for t in range(MAXL - MINL)]


def group_rows(y):
    return 1 if y == MINL else 2 ** (y - MINL - 1)


GROUP_UNITS = [group_rows(y) * BAND_UNITS[b - MINL] for b, y in GROUPS]
TOTAL_UNITS = sum(GROUP_UNITS)
GROUP_OF = [[GROUPS.index((b, y)) if (b, y) in GROUPS else 0 for y in range(MINL, MAXL + 1)] for b in range(MINL, MAXL + 1)]
HEAD_GROUPS = [k for k, (b, y) in enumerate(GROUPS) if y == MINL]


def rows_at(unit, count=1):
    return pl.ds(pl.multiple_of(unit * BASE, BASE), count * BASE)


def plan_kernel(coarse, grids_each, lev_ref, out_ref):
    total_grids = lev_ref.shape[0]
    shared = []
    for b, y in GROUPS:
        holders = jnp.int32(0)
        for dev in range(total_grids // grids_each):
            held = jnp.int32(0)
            for c in range(dev * grids_each, (dev + 1) * grids_each):
                held = held | jnp.where((lev_ref[c, 0] >= b) & (lev_ref[c, 1] >= y), 1, 0)
            holders = holders + held
        shared.append(jnp.where(holders >= 2, 1, 0))
    count = jnp.int32(0)
    for k, units in enumerate(GROUP_UNITS):
        out_ref[k] = count
        count = count + shared[k] * units * coarse
    out_ref[len(GROUPS)] = count
    for k, units in enumerate(GROUP_UNITS):
        out_ref[k] = jnp.where(shared[k] == 1, out_ref[k], count)
        count = count + (1 - shared[k]) * units * coarse


def point_of(index, points):
    tier = jnp.where(index >= 4 * BASE, 4 * BASE, jnp.where(index >= 2 * BASE, 2 * BASE, BASE))
    step = jnp.where(index >= 4 * BASE, points >> 8, jnp.where(index >= 2 * BASE, points >> 7, points >> 6))
    fine = index >= BASE
    place = jnp.where(fine, (2 * (index - tier) + 1) * step, index * (points >> MINL))
    return place, jnp.where(fine, step, 0), fine


def front_kernel(dom_shift, lev_ref, vel_ref, rate_ref, v_ref, s_ref, u_ref, first_ref, last_ref):
    g = pl.program_id(0)
    lx = lev_ref[g, 0]
    points = jnp.int32(1) << lx
    live = jnp.int32(1) << (lx + lev_ref[g, 1] - dom_shift)
    nu = vel_ref[g, 0] * points.astype(jnp.float32) / LINE
    centre = 1.0 - nu * nu
    ahead = 0.5 * nu * nu - 0.5 * nu
    behind = 0.5 * nu * nu + 0.5 * nu
    damp = 1.0 - TAU * rate_ref[g]
    p = lax.broadcasted_iota(jnp.int32, (LINE, LINE), 0)
    q = lax.broadcasted_iota(jnp.int32, (LINE, LINE), 1)
    wrap = points - 1
    place, step, fine = point_of(p & wrap, points)
    same = (p >> lx) == (q >> lx)
    off = ((q & wrap) - place) & wrap
    lower = (off + step) & wrap
    upper = (off - step) & wrap
    half = jnp.where(fine, -0.5, 0.0)

    def adv(d):
        return jnp.where(d == 0, centre, jnp.where(d == 1, ahead, jnp.where(d == wrap, behind, 0.0)))

    def one(d):
        return jnp.where(d == 0, 1.0, 0.0)

    mat_v = jnp.where(same, damp * (adv(off) + half * (adv(lower) + adv(upper))), 0.0)
    mat_s = jnp.where(same, TAU * (one(off) + half * (one(lower) + one(upper))), 0.0)
    nt = (((1,), (1,)), ((), ()))
    last_block = jnp.maximum(live // LINE - 1, 0)
    for block in range(v_ref.shape[2] // LINE):
        @pl.when(block <= last_block)
        def _():
            cut = slice(block * LINE, (block + 1) * LINE)
            res = lax.dot_general(mat_v, v_ref[0, :, cut], nt, precision=EXACT, preferred_element_type=jnp.float32)
            res = res + lax.dot_general(mat_s, s_ref[0, :, cut], nt, precision=EXACT, preferred_element_type=jnp.float32)
            u_ref[0, cut, :] = res
            if block == 0:
                first_ref[0] = res

            @pl.when(block == last_block)
            def _():
                last_ref[0] = res


def y_coefs(nu):
    return 1.0 - nu * nu, 0.5 * nu * nu - 0.5 * nu, 0.5 * nu * nu + 0.5 * nu


def slot_of(start_ref, seg_shift, y, xu):
    inner = y & ((1 << seg_shift) - 1)
    step = inner & -inner
    step_shift = jnp.where(step >= 4, 2, jnp.where(step >= 2, 1, 0))
    ylev = jnp.where(inner == 0, 0, seg_shift - step_shift)
    index = jnp.where(inner == 0, y >> seg_shift, y >> (step_shift + 1))
    band = jnp.where(xu >= 4, 3, jnp.where(xu >= 2, 2, xu))
    group = jnp.where(band == 0, ylev, jnp.where(band == 1, 4 + ylev, jnp.where(band == 2, 7 + ylev, 9)))
    width_shift = jnp.where(band >= 2, band - 1, 0)
    first = jnp.where(band >= 2, 1 << width_shift, band)
    return start_ref[group] + (index << width_shift) + xu - first, step


def middle_kernel(dom_shift, lev_ref, vel_ref, coef_ref, start_ref, u_ref, next_ref, prev_ref, t_ref, ext, mov):
    g = pl.program_id(0)
    lx, ly = lev_ref[g, 0], lev_ref[g, 1]
    live = jnp.int32(1) << (lx + ly - dom_shift)
    units = live // BASE
    x_shift = lx - MINL
    nx = jnp.int32(1) << x_shift
    seg_shift = ly - MINL
    nu = vel_ref[g, 1] * (jnp.int32(1) << ly).astype(jnp.float32) / LINE
    centre, ahead, behind = y_coefs(nu)
    weight = coef_ref[g].astype(jnp.float32)
    halo_units = next_ref.shape[1] // BASE

    @pl.when(g == 0)
    def _():
        t_ref[...] = jnp.zeros_like(t_ref)

    prev_first = jnp.where(live < LINE, units, halo_units) - nx

    def take_prev(i, _):
        ext[rows_at(i), :] = prev_ref[0, rows_at(prev_first + i), :]
        return 0

    def take_own(i, _):
        ext[rows_at(nx + i), :] = u_ref[0, rows_at(i), :]
        return 0

    def take_next(i, _):
        ext[rows_at(nx + units + i), :] = next_ref[0, rows_at(i), :]
        return 0

    lax.fori_loop(0, nx, take_prev, 0)
    lax.fori_loop(0, units, take_own, 0)
    lax.fori_loop(0, jnp.minimum(2 * nx, jnp.minimum(units, halo_units)), take_next, 0)

    def step_y(i, _):
        mov[rows_at(i), :] = centre * ext[rows_at(i + nx), :] + ahead * ext[rows_at(i + 2 * nx), :] + behind * ext[rows_at(i), :]
        return 0

    lax.fori_loop(0, jnp.where(seg_shift > 0, units + nx, units), step_y, 0)

    def surplus(i, _):
        y, xu = i >> x_shift, i & (nx - 1)
        slot, step = slot_of(start_ref, seg_shift, y, xu)
        away = step << x_shift
        half = jnp.where(step > 0, 0.5, 0.0)
        value = mov[rows_at(i), :] - half * (mov[rows_at(i - away), :] + mov[rows_at(i + away), :])
        t_ref[rows_at(slot), :] = t_ref[rows_at(slot), :] + weight * value
        return 0

    lax.fori_loop(0, units, surplus, 0)


def pack_kernel(coarse, start_ref, t_ref, tail_ref, head_ref, sems):
    copies = []
    at = 0
    for k, (b, y) in enumerate(GROUPS):
        width = BAND_UNITS[b - MINL]
        last = start_ref[k] + (coarse * group_rows(y) - 1) * width
        copies.append((rows_at(last, width), tail_ref, slice(at * BASE, (at + width) * BASE)))
        at += width
    at = 0
    for k in HEAD_GROUPS:
        width = BAND_UNITS[GROUPS[k][0] - MINL]
        copies.append((rows_at(start_ref[k], width), head_ref, slice(at * BASE, (at + width) * BASE)))
        at += width
    moves = [pltpu.make_async_copy(t_ref.at[src, :], dst.at[cut, :], sems.at[n]) for n, (src, dst, cut) in enumerate(copies)]
    for move in moves:
        move.start()
    for move in moves:
        move.wait()


def back_kernel(dom_shift, lev_ref, vel_ref, start_ref, t_ref, tail_ref, head_ref, out_ref, val, comb):
    g = pl.program_id(0)
    lx, ly = lev_ref[g, 0], lev_ref[g, 1]
    live = jnp.int32(1) << (lx + ly - dom_shift)
    units = live // BASE
    x_shift = lx - MINL
    points = jnp.int32(1) << lx
    nx = jnp.int32(1) << x_shift
    seg_shift = ly - MINL
    nu = vel_ref[g, 1] * (jnp.int32(1) << ly).astype(jnp.float32) / LINE
    centre, ahead, behind = y_coefs(nu)

    def gather(i, _):
        slot, _step = slot_of(start_ref, seg_shift, i >> x_shift, i & (nx - 1))
        val[rows_at(nx + i), :] = t_ref[rows_at(slot), :]
        return 0

    lax.fori_loop(0, units, gather, 0)

    def edges(xu, _):
        after = val[rows_at(nx + xu), :]
        band = jnp.where(xu >= 4, 3, jnp.where(xu >= 2, 2, xu))
        width = jnp.where(band >= 2, 1 << (band - 1), 1)
        base = jnp.where(band == 0, 0, jnp.where(band == 1, 4 + xu - 1, jnp.where(band == 2, 7 + xu - 2, 11 + xu - 4)))

        def finer(tier, row):
            return tail_ref[rows_at(base + tier * width), :] + 0.5 * (row + after)

        val[rows_at(xu), :] = lax.fori_loop(1, seg_shift + 1, finer, tail_ref[rows_at(base), :])
        val[rows_at(nx + units + xu), :] = head_ref[rows_at(xu), :]
        return 0

    lax.fori_loop(0, nx, edges, 0)

    def tier_loop(tier, _):
        step_shift = seg_shift - tier
        away = jnp.int32(1) << (step_shift + x_shift)

        def lift(j, _):
            y = ((j >> x_shift) * 2 + 1) << step_shift
            i = nx + (y << x_shift) + (j & (nx - 1))
            val[rows_at(i), :] = val[rows_at(i), :] + 0.5 * (val[rows_at(i - away), :] + val[rows_at(i + away), :])
            return 0

        lax.fori_loop(0, units >> (step_shift + 1), lift, 0)
        return 0

    lax.fori_loop(1, seg_shift + 1, tier_loop, 0)

    def step_y(i, _):
        comb[rows_at(i), :] = centre * val[rows_at(i + nx), :] + ahead * val[rows_at(i + 2 * nx), :] + behind * val[rows_at(i), :]
        return 0

    lax.fori_loop(0, units, step_y, 0)

    def clear(i, _):
        comb[rows_at(i), :] = jnp.zeros((BASE, comb.shape[1]), jnp.float32)
        return 0

    lax.fori_loop(units, comb.shape[0] // BASE, clear, 0)

    p = lax.broadcasted_iota(jnp.int32, (LINE, LINE), 0)
    q = lax.broadcasted_iota(jnp.int32, (LINE, LINE), 1)
    wrap = points - 1
    place, step, fine = point_of(p & wrap, points)
    reach = jnp.where(fine, step, points >> MINL)
    inverse = jnp.where(fine, jnp.where(reach == 4, 0.25, jnp.where(reach == 2, 0.5, 1.0)), 1.0 / (points >> MINL).astype(jnp.float32))
    off = ((q & wrap) - place) & wrap
    apart = jnp.minimum(off, points - off)
    hat = jnp.maximum(0.0, 1.0 - apart.astype(jnp.float32) * inverse)
    mat = jnp.where((p >> lx) == (q >> lx), hat, 0.0)
    tn = (((0,), (0,)), ((), ()))
    for block in range(out_ref.shape[2] // LINE):
        cut = slice(block * LINE, (block + 1) * LINE)

        @pl.when(block * LINE < live)
        def _():
            out_ref[0, :, cut] = lax.dot_general(comb[cut, :], mat, tn, precision=EXACT, preferred_element_type=jnp.float32)

        @pl.when(block * LINE >= live)
        def _():
            out_ref[0, :, cut] = jnp.zeros((out_ref.shape[1], LINE), jnp.float32)


def sum_line(parts):
    count = lax.axis_size("grid")
    if count == 1:
        return parts
    if count % 2:
        return [lax.psum(part, "grid") for part in parts]
    half = count // 2
    z = lax.axis_index("grid")
    held = list(parts)
    for i in range(half - 1):
        held = [part + lax.ppermute(part, "grid", [(i, i + 1), (count - 1 - i, count - 2 - i)]) for part in held]
    held = [part + lax.ppermute(part, "grid", [(half - 1, half), (half, half - 1)]) for part in held]
    for i in range(half - 2, -1, -1):
        takes = (z == i) | (z == count - 1 - i)
        held = [jnp.where(takes, lax.ppermute(part, "grid", [(i + 1, i), (count - 2 - i, count - 1 - i)]), part) for part in held]
    return held


def sum_shared(sums, sizes, which, coarse):
    def branch(size, pieces):
        def run(t):
            bounds = [size * k // pieces * coarse * BASE for k in range(pieces + 1)]
            parts = sum_line([t[a:b] for a, b in zip(bounds, bounds[1:])])
            for a, part in zip(bounds, parts):
                t = lax.dynamic_update_slice(t, part, (a, 0))
            return t

        return run

    return lax.switch(which, [branch(size, 4) for size in sizes], sums)


SMEM = pl.BlockSpec(memory_space=pltpu.SMEM)


def whole(shape):
    return pl.BlockSpec(shape, lambda g: (0,) * len(shape))


def per_grid(shape):
    return pl.BlockSpec((1,) + shape, lambda g: (g, 0, 0))


def local(nodal_values, source_term, velocity, react_rate, levels, comb_coefs):
    grids, other, block_len = nodal_values.shape
    dom = lax.axis_size("dom")
    dom_shift = dom.bit_length() - 1
    coarse = BASE // dom
    params = pltpu.CompilerParams(vmem_limit_bytes=VMEM_BYTES)
    f32 = jnp.float32
    all_levels = lax.all_gather(levels, "grid", tiled=True)

    values, first, last = pl.pallas_call(
        functools.partial(front_kernel, dom_shift),
        grid=(grids,),
        in_specs=[SMEM, SMEM, SMEM, per_grid((other, block_len)), per_grid((other, block_len))],
        out_specs=[per_grid((block_len, other)), per_grid((LINE, other)), per_grid((LINE, other))],
        out_shape=[
            jax.ShapeDtypeStruct((grids, block_len, other), f32),
            jax.ShapeDtypeStruct((grids, LINE, other), f32),
            jax.ShapeDtypeStruct((grids, LINE, other), f32),
        ],
        compiler_params=params,
        name="front",
    )(levels, velocity, react_rate, nodal_values, source_term)

    to_next = [(i, (i + 1) % dom) for i in range(dom)]
    to_prev = [(i, (i - 1) % dom) for i in range(dom)]
    after = lax.ppermute(first, "dom", to_prev)
    before = lax.ppermute(last, "dom", to_next)

    starts = pl.pallas_call(
        functools.partial(plan_kernel, coarse, grids),
        in_specs=[SMEM],
        out_specs=SMEM,
        out_shape=jax.ShapeDtypeStruct((len(GROUPS) + 1,), jnp.int32),
        name="plan",
    )(all_levels)

    sum_rows = TOTAL_UNITS * coarse * BASE
    sums = pl.pallas_call(
        functools.partial(middle_kernel, dom_shift),
        grid=(grids,),
        in_specs=[SMEM, SMEM, SMEM, SMEM, per_grid((block_len, other)), per_grid((LINE, other)), per_grid((LINE, other))],
        out_specs=whole((sum_rows, other)),
        out_shape=jax.ShapeDtypeStruct((sum_rows, other), f32),
        scratch_shapes=[pltpu.VMEM((block_len + 3 * LINE, other), f32), pltpu.VMEM((block_len + LINE, other), f32)],
        compiler_params=params,
        name="middle",
    )(levels, velocity, comb_coefs, starts, values, after, before)

    sizes = [5, 6, 7, 8, 9, 10, 11, 12, 13, 14, 16, TOTAL_UNITS]
    limits = jnp.asarray([size * coarse for size in sizes[:-1]], jnp.int32)
    which = jnp.sum((starts[len(GROUPS)] > limits).astype(jnp.int32))
    sums = sum_shared(sums, sizes, which, coarse)

    any_space = pl.BlockSpec(memory_space=pl.ANY)
    tail_rows = sum(BAND_UNITS[b - MINL] for b, _ in GROUPS) * BASE
    head_rows = sum(BAND_UNITS) * BASE
    tail, head = pl.pallas_call(
        functools.partial(pack_kernel, coarse),
        in_specs=[SMEM, any_space],
        out_specs=[any_space, any_space],
        out_shape=[jax.ShapeDtypeStruct((tail_rows, other), f32), jax.ShapeDtypeStruct((head_rows, other), f32)],
        scratch_shapes=[pltpu.SemaphoreType.DMA((len(GROUPS) + len(HEAD_GROUPS),))],
        compiler_params=params,
        name="pack",
    )(starts, sums)
    tail = lax.ppermute(tail, "dom", to_next)
    head = lax.ppermute(head, "dom", to_prev)

    return pl.pallas_call(
        functools.partial(back_kernel, dom_shift),
        grid=(grids,),
        in_specs=[SMEM, SMEM, SMEM, whole((sum_rows, other)), whole((tail_rows, other)), whole((head_rows, other))],
        out_specs=per_grid((other, block_len)),
        out_shape=jax.ShapeDtypeStruct((grids, other, block_len), f32),
        scratch_shapes=[pltpu.VMEM((block_len + 2 * LINE, other), f32), pltpu.VMEM((block_len, other), f32)],
        compiler_params=params,
        name="back",
    )(levels, velocity, starts, sums, tail, head)


def solution(mesh):
    in_specs = (
        P("grid", None, "dom"),
        P("grid", None, "dom"),
        P("grid", None),
        P("grid"),
        P("grid", None),
        P("grid"),
    )
    return jax.shard_map(local, mesh=mesh, in_specs=in_specs, out_specs=P("grid", None, "dom"), check_vma=False)
```

time: 363 us -> 120 us (0.33); the launches traced: 356 us -> 118 us
  matrix products: 126 us -> 0 us
  waiting for transfers between devices: 152 us -> 48 us
  local copies, waits for them, and re-layouts: 42.7 us -> 6.79 us
  Pallas kernels: 0 us -> 19.5 us
  starting transfers between devices: 10.1 us -> 25.3 us
  between operations: 14.2 us -> 0.64 us
  blocking collectives: 0 us -> 11.7 us
  other arithmetic: 10.5 us -> 5.85 us
    dot_general x20 -> x0, matrix products: 126 us -> none  [the longest x17 82.4 us: pick_last(): jnp.einsum('zrs,zsd->zrd', source_arr, table, precision=lax.Precision.HIG...]
    psum x1 -> x0, waiting for transfers between devices: 106 us -> none  [combine_grids(): return lax.psum(partial_sum, 'grid')]
    ppermute x0 -> x16, waiting for transfers between devices: none -> 48 us  [the longest x4 24 us: sum_line(): lax.ppermute(part, 'grid', [(i + 1, i), (count - 2 - i, count - 1 - i)])]
    all_to_all x2 -> x0, waiting for transfers between devices: 45.7 us -> none  [local(): lax.all_to_all(outgoing, 'dom', split_axis=2, concat_axis=2, tiled=True)]
    gather x6 -> x0, local copies, waits for them, and re-layouts: 39.4 us -> none  [the longest x4 26.8 us: hier_gather(): jnp.take(order_table, position)]
    ppermute x0 -> x16, starting transfers between devices: none -> 25.3 us  [the longest x1 9.51 us: local(): tail = lax.ppermute(tail, 'dom', to_next)]
    pallas_call x0 -> x5, Pallas kernels: none -> 19.5 us  [the longest x1 6.65 us: local(): pl.pallas_call(functools.partial(back_kernel, dom_shift), grid=(grids,),...]
    all_gather x0 -> x1, blocking collectives: none -> 11.7 us  [local(): all_levels = lax.all_gather(levels, 'grid', tiled=True)]
  transfers between devices with their start and end apart: 3 -> 16, of which waited for: 3 -> 8; matrix products, arithmetic and copies ran while one was open for 0% -> 4% of each run, Pallas kernels for 0% -> 1%
where the time goes in v1:
time: 120 us; the launch traced here: 118 us
  waiting for transfers between devices  48 us (40%)
  starting transfers between devices  25.3 us (21%)
  Pallas kernels  19.5 us (16%)
  blocking collectives  11.7 us (10%)
  local copies, waits for them, and re-layouts  6.79 us (6%)
  other arithmetic  5.85 us (5%)
    ppermute x4, waiting for transfers between devices, sum_line(): lax.ppermute(part, 'grid', [(i + 1, i), (count - 2 - i, count - 1 - i)])  24 us
    ppermute x4, waiting for transfers between devices, sum_line(): lax.ppermute(part, 'grid', [(i, i + 1), (count - 1 - i, count - 2 - i)])  15.8 us
    all_gather x1, blocking collectives, local(): all_levels = lax.all_gather(levels, 'grid', tiled=True)  11.7 us
    ppermute x1, starting transfers between devices, local(): tail = lax.ppermute(tail, 'dom', to_next)  9.51 us
    ppermute x1, waiting for transfers between devices, local(): head = lax.ppermute(head, 'dom', to_prev)  8.23 us
    pallas_call x1, Pallas kernels, local(): pl.pallas_call(functools.partial(back_kernel, dom_shift), grid=(grids,),...  6.65 us
    pallas_call x1, Pallas kernels, local(): pl.pallas_call(functools.partial(front_kernel, dom_shift), grid=(grids,),...  5.53 us
    ppermute x4, starting transfers between devices, sum_line(): lax.ppermute(part, 'grid', [(i, i + 1), (count - 1 - i, count - 2 - i)])  5.35 us
  transfers between devices with their start and end apart: 16, of which 8 were waited for; matrix products, arithmetic and copies ran while one was open for 4% of the time, Pallas kernels for 1%

profile of v1, /device:TPU:1, one launch (start us, length us, event | category | flops | bytes accessed | tf_op | source)
XLA Modules:
  0.0 118.0 jit_solution(9335455771260648458)
XLA Ops:
  0.0 1.6 %copy-done = f32[2,256,1024]{2,1,0:T(8,128)S(1)} copy-done((f32[2,256,1024]{2,1,0:T(8,128)S(1)}, f32[2,256,1024]{2,1,0:T(8,128)}, u32[]{:S(2)}) %copy-start) | copy-done | bytes 2097176
  1.6 0.7 copy-done.1
  2.3 0.7 copy-done.3
  3.0 0.7 copy-done.7
  3.6 5.5 %front.1 = (f32[2,1024,256]{2,1,0:T(8,128)S(1)}, f32[2,256,256]{2,1,0:T(8,128)}, f32[2,256,256]{2,1,0:T(8,128)}) custom-call(s32[2,2]{1,0:T(2,128)S(1)} %copy-done.1, f32[2,2]{1,0:T(2,128)S(1)} %copy-done.3, f32[2]{0:T(128)S(1)} %copy-done.7, f32[2,256,1024]{2,1,0:T(8,128)S(1)} %copy-done, f32[2,256,1024]{2,1,0:T(8,128)} %s_ref.1), custom_call_target="tpu_custom_call" | custom-call | tf_op jit(solution)/shard_map/front/pallas_call | solution.py:339
  9.2 0.1 collective-permute-start.144
  9.2 2.5 %collective-permute-start.145 = (f32[2,256,256]{2,1,0:T(8,128)}, f32[2,256,256]{2,1,0:T(8,128)S(1)}, u32[]{:S(2)}, u32[]{:S(2)}) collective-permute-start(f32[2,256,256]{2,1,0:T(8,128)} %get-tuple-element.37), channel_id=1, source_target_pairs={{0,1},{1,2},{2,3},{3,4},{4,5},{5,6},{6,7},{7,0},{8,9},{9,10},{10,1... | collective-permute-start | bytes 1572872 | tf_op jit(solution)/shard_map/ppermute | solution.py:356
  11.8 11.7 %all-gather = s32[4,2,2]{2,1,0:T(2,128)} all-gather(s32[1,2,2]{2,1,0:T(2,128)S(1)} %bitcast.3), channel_id=1, replica_groups=mesh['grid'=4,'dom'=8] {'grid'}, dimensions={0}, use_global_device_ids=true | all-gather | bytes 80 | tf_op jit(solution)/shard_map/all_gather | solution.py:337
  23.5 1.4 %plan.1.start_ref = s32[11]{0:T(128)} custom-call(s32[8,2]{1,0:T(8,128)} %bitcast.4), custom_call_target="tpu_custom_call" | custom-call | tf_op jit(solution)/shard_map/plan/pallas_call | solution.py:358
  24.9 1.3 %slice.147 = s32[1]{0:T(128)} slice(s32[11]{0:T(128)} %plan.1.start_ref), slice={[10:11]} | slice | bytes 8 | tf_op jit(solution)/shard_map/slice | solution.py:380
  26.2 1.2 %fusion = s32[]{:T(128)} fusion(s32[11]{0:T(128)S(1)} %copy-done.9, s32[]{:T(128)} %bitcast.2), kind=kLoop, calls=%fused_computation.97 | loop fusion | flops 32 | bytes 52 | tf_op jit(solution)/shard_map/reduce_sum | solution.py:380
  28.0 0.0 collective-permute-done.144.next_ref
  28.0 0.0 collective-permute-done.145.prev_ref
  28.1 0.6 copy-done.5
  28.7 4.0 %middle.1 = f32[2560,256]{1,0:T(8,128)} custom-call(s32[2,2]{1,0:T(2,128)S(1)} %copy-done.2, f32[2,2]{1,0:T(2,128)S(1)} %copy-done.4, s32[2]{0:T(128)S(1)} %copy-done.8, s32[11]{0:T(128)S(1)} %copy-done.5, f32[2,1024,256]{2,1,0:T(8,128)S(1)} %get-tuple-element.35.u_ref, f32[2,256,256]{2,1,0:T(8,128)S(1)} %collective-permute-done.144.next_ref, ...), custom_call_target="tpu_custom_call" | custom-call | tf_op jit(solution)/shard_map/middle/pallas_call | solution.py:367
  32.7 59.0 %conditional.1 = (f32[2560,256]{1,0:T(8,128)}) conditional(s32[]{:T(128)} %clamp.3, f32[2560,256]{1,0:T(8,128)} %middle.1, f32[2560,256]{1,0:T(8,128)} %middle.1, f32[2560,256]{1,0:T(8,128)} %middle.1, f32[2560,256]{1,0:T(8,128)} %middle.1, f32[2560,256]{1,0:T(8,128)} %middle.1, f32[2560,256]{1,0:T(8,128)} %middle.1, ...), branch_computations={%region_1.2_spmd, %region_2.3_spmd, %region_3.4_spmd, %region_4.5_... | conditional | flops 1966086 | bytes 60293660 | solution.py:316
  32.7 1.3 %fusion.5 = (f32[256,256]{1,0:T(8,128)S(1)}, f32[256,256]{1,0:T(8,128)S(1)}, f32[256,256]{1,0:T(8,128)S(1)}, f32[256,256]{1,0:T(8,128)S(1)}) fusion(f32[2560,256]{1,0:T(8,128)} %param.3), kind=kLoop, calls=%fused_computation.102 | loop fusion | bytes 2097152 | tf_op jit(solution)/shard_map/cond/branch_3_fun/slice | solution.py:309
  34.0 1.4 %collective-permute-start.45 = (f32[256,256]{1,0:T(8,128)S(1)}, f32[256,256]{1,0:T(8,128)S(1)}, u32[]{:S(2)}, u32[]{:S(2)}) collective-permute-start(f32[256,256]{1,0:T(8,128)S(1)} %get-tuple-element.64), channel_id=1, source_target_pairs={{0,8},{24,16},{1,9},{25,17},{2,10},{26,18},{3,11},{27,19},{4,12},{... | collective-permute-start | bytes 786440 | tf_op jit(solution)/shard_map/cond/branch_3_fun/ppermute | solution.py:297
  35.4 1.3 %collective-permute-start.36 = (f32[256,256]{1,0:T(8,128)S(1)}, f32[256,256]{1,0:T(8,128)S(1)}, u32[]{:S(2)}, u32[]{:S(2)}) collective-permute-start(f32[256,256]{1,0:T(8,128)S(1)} %get-tuple-element.67), channel_id=1, source_target_pairs={{0,8},{24,16},{1,9},{25,17},{2,10},{26,18},{3,11},{27,19},{4,12},{... | collective-permute-start | bytes 786440 | tf_op jit(solution)/shard_map/cond/branch_3_fun/ppermute | solution.py:297
  36.7 1.3 %collective-permute-start.39 = (f32[256,256]{1,0:T(8,128)S(1)}, f32[256,256]{1,0:T(8,128)S(1)}, u32[]{:S(2)}, u32[]{:S(2)}) collective-permute-start(f32[256,256]{1,0:T(8,128)S(1)} %get-tuple-element.66), channel_id=1, source_target_pairs={{0,8},{24,16},{1,9},{25,17},{2,10},{26,18},{3,11},{27,19},{4,12},{... | collective-permute-start | bytes 786440 | tf_op jit(solution)/shard_map/cond/branch_3_fun/ppermute | solution.py:297
  38.0 1.3 %collective-permute-start.42 = (f32[256,256]{1,0:T(8,128)S(1)}, f32[256,256]{1,0:T(8,128)S(1)}, u32[]{:S(2)}, u32[]{:S(2)}) collective-permute-start(f32[256,256]{1,0:T(8,128)S(1)} %get-tuple-element.65), channel_id=1, source_target_pairs={{0,8},{24,16},{1,9},{25,17},{2,10},{26,18},{3,11},{27,19},{4,12},{... | collective-permute-start | bytes 786440 | tf_op jit(solution)/shard_map/cond/branch_3_fun/ppermute | solution.py:297
  39.3 0.0 collective-permute-done.45
  39.3 4.5 %collective-permute-done.36 = f32[256,256]{1,0:T(8,128)S(1)} collective-permute-done((f32[256,256]{1,0:T(8,128)S(1)}, f32[256,256]{1,0:T(8,128)S(1)}, u32[]{:S(2)}, u32[]{:S(2)}) %collective-permute-start.36) | collective-permute-done | bytes 262176 | tf_op jit(solution)/shard_map/cond/branch_3_fun/ppermute | solution.py:297
  43.9 5.6 %collective-permute-done.39 = f32[256,256]{1,0:T(8,128)S(1)} collective-permute-done((f32[256,256]{1,0:T(8,128)S(1)}, f32[256,256]{1,0:T(8,128)S(1)}, u32[]{:S(2)}, u32[]{:S(2)}) %collective-permute-start.39) | collective-permute-done | bytes 262176 | tf_op jit(solution)/shard_map/cond/branch_3_fun/ppermute | solution.py:297
  49.5 5.6 %collective-permute-done.42 = f32[256,256]{1,0:T(8,128)S(1)} collective-permute-done((f32[256,256]{1,0:T(8,128)S(1)}, f32[256,256]{1,0:T(8,128)S(1)}, u32[]{:S(2)}, u32[]{:S(2)}) %collective-permute-start.42) | collective-permute-done | bytes 262176 | tf_op jit(solution)/shard_map/cond/branch_3_fun/ppermute | solution.py:297
  55.1 1.4 %slice_add_fusion.12 = (f32[256,256]{1,0:T(8,128)S(1)}, f32[256,256]{1,0:T(8,128)S(1)}, f32[256,256]{1,0:T(8,128)S(1)}, f32[256,256]{1,0:T(8,128)S(1)}) fusion(f32[256,256]{1,0:T(8,128)S(1)} %collective-permute-done.45, f32[2560,256]{1,0:T(8,128)} %param.3, f32[256,256]{1,0:T(8,128)S(1)} %collective-permute-done.36, ...), kind=kLoop, calls=%fused_computation.28 | loop fusion | flops 262144 | bytes 3145728 | tf_op jit(solution)/shard_map/cond/branch_3_fun/add | solution.py:297
  56.5 0.7 collective-permute-start.37
  57.2 0.7 collective-permute-start.40
  57.9 0.7 collective-permute-start.43
  58.6 0.7 collective-permute-start.46
  59.3 0.0 collective-permute-done.37
  59.3 1.3 %collective-permute-start.38 = (f32[256,256]{1,0:T(8,128)S(1)}, f32[256,256]{1,0:T(8,128)S(1)}, u32[]{:S(2)}, u32[]{:S(2)}) collective-permute-start(f32[256,256]{1,0:T(8,128)S(1)} %add.217), channel_id=1, source_target_pairs={{8,0},{16,24},{9,1},{17,25},{10,2},{18,26},{11,3},{19,27},{12,4},{... | collective-permute-start | bytes 786440 | tf_op jit(solution)/shard_map/cond/branch_3_fun/ppermute | solution.py:301
  60.7 1.3 %collective-permute-start.41 = (f32[256,256]{1,0:T(8,128)S(1)}, f32[256,256]{1,0:T(8,128)S(1)}, u32[]{:S(2)}, u32[]{:S(2)}) collective-permute-start(f32[256,256]{1,0:T(8,128)S(1)} %add.219), channel_id=1, source_target_pairs={{8,0},{16,24},{9,1},{17,25},{10,2},{18,26},{11,3},{19,27},{12,4},{... | collective-permute-start | bytes 786440 | tf_op jit(solution)/shard_map/cond/branch_3_fun/ppermute | solution.py:301
  62.1 1.3 %collective-permute-start.44 = (f32[256,256]{1,0:T(8,128)S(1)}, f32[256,256]{1,0:T(8,128)S(1)}, u32[]{:S(2)}, u32[]{:S(2)}) collective-permute-start(f32[256,256]{1,0:T(8,128)S(1)} %add.221), channel_id=1, source_target_pairs={{8,0},{16,24},{9,1},{17,25},{10,2},{18,26},{11,3},{19,27},{12,4},{... | collective-permute-start | bytes 786440 | tf_op jit(solution)/shard_map/cond/branch_3_fun/ppermute | solution.py:301
  63.4 1.3 %collective-permute-start.47 = (f32[256,256]{1,0:T(8,128)S(1)}, f32[256,256]{1,0:T(8,128)S(1)}, u32[]{:S(2)}, u32[]{:S(2)}) collective-permute-start(f32[256,256]{1,0:T(8,128)S(1)} %add.223), channel_id=1, source_target_pairs={{8,0},{16,24},{9,1},{17,25},{10,2},{18,26},{11,3},{19,27},{12,4},{... | collective-permute-start | bytes 786440 | tf_op jit(solution)/shard_map/cond/branch_3_fun/ppermute | solution.py:301
  64.7 9.9 %collective-permute-done.38 = f32[256,256]{1,0:T(8,128)S(1)} collective-permute-done((f32[256,256]{1,0:T(8,128)S(1)}, f32[256,256]{1,0:T(8,128)S(1)}, u32[]{:S(2)}, u32[]{:S(2)}) %collective-permute-start.38) | collective-permute-done | bytes 262176 | tf_op jit(solution)/shard_map/cond/branch_3_fun/ppermute | solution.py:301
  74.6 0.8 select_dynamic-update-slice_fusion.15
  75.4 3.1 %collective-permute-done.41 = f32[256,256]{1,0:T(8,128)S(1)} collective-permute-done((f32[256,256]{1,0:T(8,128)S(1)}, f32[256,256]{1,0:T(8,128)S(1)}, u32[]{:S(2)}, u32[]{:S(2)}) %collective-permute-start.41) | collective-permute-done | bytes 262176 | tf_op jit(solution)/shard_map/cond/branch_3_fun/ppermute | solution.py:301
  78.4 0.7 select_dynamic-update-slice_fusion.14
  79.2 5.6 %collective-permute-done.44 = f32[256,256]{1,0:T(8,128)S(1)} collective-permute-done((f32[256,256]{1,0:T(8,128)S(1)}, f32[256,256]{1,0:T(8,128)S(1)}, u32[]{:S(2)}, u32[]{:S(2)}) %collective-permute-start.44) | collective-permute-done | bytes 262176 | tf_op jit(solution)/shard_map/cond/branch_3_fun/ppermute | solution.py:301
  84.8 0.7 select_dynamic-update-slice_fusion.13
  85.5 5.5 %collective-permute-done.47 = f32[256,256]{1,0:T(8,128)S(1)} collective-permute-done((f32[256,256]{1,0:T(8,128)S(1)}, f32[256,256]{1,0:T(8,128)S(1)}, u32[]{:S(2)}, u32[]{:S(2)}) %collective-permute-start.47) | collective-permute-done | bytes 262176 | tf_op jit(solution)/shard_map/cond/branch_3_fun/ppermute | solution.py:301
  91.0 0.8 select_dynamic-update-slice_fusion.12
  91.7 1.9 %pack.1 = (f32[480,256]{1,0:T(8,128)S(1)}, f32[256,256]{1,0:T(8,128)S(1)}) custom-call(s32[11]{0:T(128)S(1)} %copy-done.6, f32[2560,256]{1,0:T(8,128)} %get-tuple-element.126.t_ref), custom_call_target="tpu_custom_call" | custom-call | tf_op jit(solution)/shard_map/pack/pallas_call | solution.py:386
  93.6 9.5 %collective-permute-start.146 = (f32[480,256]{1,0:T(8,128)S(1)}, f32[480,256]{1,0:T(8,128)S(1)}, u32[]{:S(2)}, u32[]{:S(2)}) collective-permute-start(f32[480,256]{1,0:T(8,128)S(1)} %get-tuple-element.38), channel_id=1, source_target_pairs={{0,1},{1,2},{2,3},{3,4},{4,5},{5,6},{6,7},{7,0},{8,9},{9,10},{10,1... | collective-permute-start | bytes 1474568 | tf_op jit(solution)/shard_map/ppermute | solution.py:395
  103.1 0.0 collective-permute-start.147
  103.1 8.2 %collective-permute-done.147.head_ref = f32[256,256]{1,0:T(8,128)S(1)} collective-permute-done((f32[256,256]{1,0:T(8,128)S(1)}, f32[256,256]{1,0:T(8,128)S(1)}, u32[]{:S(2)}, u32[]{:S(2)}) %collective-permute-start.147) | collective-permute-done | bytes 262176 | tf_op jit(solution)/shard_map/ppermute | solution.py:396
  111.4 6.6 %back.1 = f32[2,256,1024]{2,1,0:T(8,128)} custom-call(s32[2,2]{1,0:T(2,128)S(1)} %copy-done.2, f32[2,2]{1,0:T(2,128)S(1)} %copy-done.4, s32[11]{0:T(128)S(1)} %copy-done.6, f32[2560,256]{1,0:T(8,128)} %get-tuple-element.126.t_ref, f32[480,256]{1,0:T(8,128)S(1)} %collective-permute-done.146.tail_ref, f32[256,256]{1,0:T(8,128)S(1)} %collective-permute-done.147.head_ref), custom_call_target="tpu_custom_call" | custom-call | tf_op jit(solution)/shard_map/back/pallas_call | solution.py:398
  (23 shorter events, 0.2 us)
Async XLA Ops:
  0.0 26.2 %copy-start.9 = (s32[11]{0:T(128)S(1)}, s32[11]{0:T(128)}, u32[]{:S(2)}) copy-start(s32[11]{0:T(128)} %constant.186.clone) | copy-start | bytes 136
  0.0 1.6 %copy-start = (f32[2,256,1024]{2,1,0:T(8,128)S(1)}, f32[2,256,1024]{2,1,0:T(8,128)}, u32[]{:S(2)}) copy-start(f32[2,256,1024]{2,1,0:T(8,128)} %v_ref.1) | copy-start | bytes 6291460
  1.6 0.7 copy-start.1
  2.3 0.7 copy-start.3
  3.0 0.7 copy-start.7
  3.6 24.4 %copy-start.2 = (s32[2,2]{1,0:T(2,128)S(1)}, s32[2,2]{1,0:T(2,128)}, u32[]{:S(2)}) copy-start(s32[2,2]{1,0:T(2,128)} %lev_ref.5) | copy-start | bytes 52
  3.6 24.4 %copy-start.4 = (f32[2,2]{1,0:T(2,128)S(1)}, f32[2,2]{1,0:T(2,128)}, u32[]{:S(2)}) copy-start(f32[2,2]{1,0:T(2,128)} %vel_ref.5) | copy-start | bytes 52
  3.6 24.4 %copy-start.8 = (s32[2]{0:T(128)S(1)}, s32[2]{0:T(128)}, u32[]{:S(2)}) copy-start(s32[2]{0:T(128)} %coef_ref.1) | copy-start | bytes 28
  9.2 18.8 %collective-permute-start.144 = (f32[2,256,256]{2,1,0:T(8,128)}, f32[2,256,256]{2,1,0:T(8,128)S(1)}, u32[]{:S(2)}, u32[]{:S(2)}) collective-permute-start(f32[2,256,256]{2,1,0:T(8,128)} %get-tuple-element.36), channel_id=1, source_target_pairs={{0,7},{1,0},{2,1},{3,2},{4,3},{5,4},{6,5},{7,6},{8,15},{9,8},{10,9... | collective-permute-start | bytes 1572872 | tf_op jit(solution)/shard_map/ppermute | solution.py:355
  9.2 18.8 %collective-permute-start.145 = (f32[2,256,256]{2,1,0:T(8,128)}, f32[2,256,256]{2,1,0:T(8,128)S(1)}, u32[]{:S(2)}, u32[]{:S(2)}) collective-permute-start(f32[2,256,256]{2,1,0:T(8,128)} %get-tuple-element.37), channel_id=1, source_target_pairs={{0,1},{1,2},{2,3},{3,4},{4,5},{5,6},{6,7},{7,0},{8,9},{9,10},{10,1... | collective-permute-start | bytes 1572872 | tf_op jit(solution)/shard_map/ppermute | solution.py:356
  28.0 0.6 copy-start.5
  32.7 59.1 %copy-start.6 = (s32[11]{0:T(128)S(1)}, s32[11]{0:T(128)}, u32[]{:S(2)}) copy-start(s32[11]{0:T(128)} %plan.1.start_ref) | copy-start | bytes 136
  34.0 5.4 %collective-permute-start.45 = (f32[256,256]{1,0:T(8,128)S(1)}, f32[256,256]{1,0:T(8,128)S(1)}, u32[]{:S(2)}, u32[]{:S(2)}) collective-permute-start(f32[256,256]{1,0:T(8,128)S(1)} %get-tuple-element.64), channel_id=1, source_target_pairs={{0,8},{24,16},{1,9},{25,17},{2,10},{26,18},{3,11},{27,19},{4,12},{... | collective-permute-start | bytes 786440 | tf_op jit(solution)/shard_map/cond/branch_3_fun/ppermute | solution.py:297
  35.4 8.5 %collective-permute-start.36 = (f32[256,256]{1,0:T(8,128)S(1)}, f32[256,256]{1,0:T(8,128)S(1)}, u32[]{:S(2)}, u32[]{:S(2)}) collective-permute-start(f32[256,256]{1,0:T(8,128)S(1)} %get-tuple-element.67), channel_id=1, source_target_pairs={{0,8},{24,16},{1,9},{25,17},{2,10},{26,18},{3,11},{27,19},{4,12},{... | collective-permute-start | bytes 786440 | tf_op jit(solution)/shard_map/cond/branch_3_fun/ppermute | solution.py:297
  36.7 12.8 %collective-permute-start.39 = (f32[256,256]{1,0:T(8,128)S(1)}, f32[256,256]{1,0:T(8,128)S(1)}, u32[]{:S(2)}, u32[]{:S(2)}) collective-permute-start(f32[256,256]{1,0:T(8,128)S(1)} %get-tuple-element.66), channel_id=1, source_target_pairs={{0,8},{24,16},{1,9},{25,17},{2,10},{26,18},{3,11},{27,19},{4,12},{... | collective-permute-start | bytes 786440 | tf_op jit(solution)/shard_map/cond/branch_3_fun/ppermute | solution.py:297
  38.0 17.1 %collective-permute-start.42 = (f32[256,256]{1,0:T(8,128)S(1)}, f32[256,256]{1,0:T(8,128)S(1)}, u32[]{:S(2)}, u32[]{:S(2)}) collective-permute-start(f32[256,256]{1,0:T(8,128)S(1)} %get-tuple-element.65), channel_id=1, source_target_pairs={{0,8},{24,16},{1,9},{25,17},{2,10},{26,18},{3,11},{27,19},{4,12},{... | collective-permute-start | bytes 786440 | tf_op jit(solution)/shard_map/cond/branch_3_fun/ppermute | solution.py:297
  56.5 2.7 %collective-permute-start.37 = (f32[256,256]{1,0:T(8,128)S(1)}, f32[256,256]{1,0:T(8,128)S(1)}, u32[]{:S(2)}, u32[]{:S(2)}) collective-permute-start(f32[256,256]{1,0:T(8,128)S(1)} %get-tuple-element.61), channel_id=1, source_target_pairs={{8,16},{16,8},{9,17},{17,9},{10,18},{18,10},{11,19},{19,11},{12,20... | collective-permute-start | bytes 786440 | tf_op jit(solution)/shard_map/cond/branch_3_fun/ppermute | solution.py:298
  57.2 3.4 %collective-permute-start.40 = (f32[256,256]{1,0:T(8,128)S(1)}, f32[256,256]{1,0:T(8,128)S(1)}, u32[]{:S(2)}, u32[]{:S(2)}) collective-permute-start(f32[256,256]{1,0:T(8,128)S(1)} %get-tuple-element.62), channel_id=1, source_target_pairs={{8,16},{16,8},{9,17},{17,9},{10,18},{18,10},{11,19},{19,11},{12,20... | collective-permute-start | bytes 786440 | tf_op jit(solution)/shard_map/cond/branch_3_fun/ppermute | solution.py:298
  57.9 4.1 %collective-permute-start.43 = (f32[256,256]{1,0:T(8,128)S(1)}, f32[256,256]{1,0:T(8,128)S(1)}, u32[]{:S(2)}, u32[]{:S(2)}) collective-permute-start(f32[256,256]{1,0:T(8,128)S(1)} %get-tuple-element.63), channel_id=1, source_target_pairs={{8,16},{16,8},{9,17},{17,9},{10,18},{18,10},{11,19},{19,11},{12,20... | collective-permute-start | bytes 786440 | tf_op jit(solution)/shard_map/cond/branch_3_fun/ppermute | solution.py:298
  58.6 4.8 %collective-permute-start.46 = (f32[256,256]{1,0:T(8,128)S(1)}, f32[256,256]{1,0:T(8,128)S(1)}, u32[]{:S(2)}, u32[]{:S(2)}) collective-permute-start(f32[256,256]{1,0:T(8,128)S(1)} %get-tuple-element.60), channel_id=1, source_target_pairs={{8,16},{16,8},{9,17},{17,9},{10,18},{18,10},{11,19},{19,11},{12,20... | collective-permute-start | bytes 786440 | tf_op jit(solution)/shard_map/cond/branch_3_fun/ppermute | solution.py:298
  59.3 15.2 %collective-permute-start.38 = (f32[256,256]{1,0:T(8,128)S(1)}, f32[256,256]{1,0:T(8,128)S(1)}, u32[]{:S(2)}, u32[]{:S(2)}) collective-permute-start(f32[256,256]{1,0:T(8,128)S(1)} %add.217), channel_id=1, source_target_pairs={{8,0},{16,24},{9,1},{17,25},{10,2},{18,26},{11,3},{19,27},{12,4},{... | collective-permute-start | bytes 786440 | tf_op jit(solution)/shard_map/cond/branch_3_fun/ppermute | solution.py:301
  60.7 17.7 %collective-permute-start.41 = (f32[256,256]{1,0:T(8,128)S(1)}, f32[256,256]{1,0:T(8,128)S(1)}, u32[]{:S(2)}, u32[]{:S(2)}) collective-permute-start(f32[256,256]{1,0:T(8,128)S(1)} %add.219), channel_id=1, source_target_pairs={{8,0},{16,24},{9,1},{17,25},{10,2},{18,26},{11,3},{19,27},{12,4},{... | collective-permute-start | bytes 786440 | tf_op jit(solution)/shard_map/cond/branch_3_fun/ppermute | solution.py:301
  62.1 22.7 %collective-permute-start.44 = (f32[256,256]{1,0:T(8,128)S(1)}, f32[256,256]{1,0:T(8,128)S(1)}, u32[]{:S(2)}, u32[]{:S(2)}) collective-permute-start(f32[256,256]{1,0:T(8,128)S(1)} %add.221), channel_id=1, source_target_pairs={{8,0},{16,24},{9,1},{17,25},{10,2},{18,26},{11,3},{19,27},{12,4},{... | collective-permute-start | bytes 786440 | tf_op jit(solution)/shard_map/cond/branch_3_fun/ppermute | solution.py:301
  63.4 27.6 %collective-permute-start.47 = (f32[256,256]{1,0:T(8,128)S(1)}, f32[256,256]{1,0:T(8,128)S(1)}, u32[]{:S(2)}, u32[]{:S(2)}) collective-permute-start(f32[256,256]{1,0:T(8,128)S(1)} %add.223), channel_id=1, source_target_pairs={{8,0},{16,24},{9,1},{17,25},{10,2},{18,26},{11,3},{19,27},{12,4},{... | collective-permute-start | bytes 786440 | tf_op jit(solution)/shard_map/cond/branch_3_fun/ppermute | solution.py:301
  93.6 17.7 %collective-permute-start.146 = (f32[480,256]{1,0:T(8,128)S(1)}, f32[480,256]{1,0:T(8,128)S(1)}, u32[]{:S(2)}, u32[]{:S(2)}) collective-permute-start(f32[480,256]{1,0:T(8,128)S(1)} %get-tuple-element.38), channel_id=1, source_target_pairs={{0,1},{1,2},{2,3},{3,4},{4,5},{5,6},{6,7},{7,0},{8,9},{9,10},{10,1... | collective-permute-start | bytes 1474568 | tf_op jit(solution)/shard_map/ppermute | solution.py:395
  103.1 8.2 %collective-permute-start.147 = (f32[256,256]{1,0:T(8,128)S(1)}, f32[256,256]{1,0:T(8,128)S(1)}, u32[]{:S(2)}, u32[]{:S(2)}) collective-permute-start(f32[256,256]{1,0:T(8,128)S(1)} %get-tuple-element.39), channel_id=1, source_target_pairs={{0,7},{1,0},{2,1},{3,2},{4,3},{5,4},{6,5},{7,6},{8,15},{9,8},{10,9... | collective-permute-start | bytes 786440 | tf_op jit(solution)/shard_map/ppermute | solution.py:396
